TPU v7x, 256 devices: a whole 4x4x8 slice. The times are simulated.
256 devices in a mesh: row: 8 (over x, z_hi), col: 32 (over y, z_lo, core).
Axes of the slice: x: 4, y: 4, z: 8 (z_hi: 2, z_lo: 4; z = z_hi * 4 + z_lo), core: 2. Of those that a mesh axis runs over, the one named last changes fastest.
Arguments:
- amplitudes: bfloat16 [8192, 65536], P('row', 'col'), may hold values from -6 to 6
- residual_in: bfloat16 [8192, 65536], P('row', 'col'), may hold values from -6 to 6
- cholesky: bfloat16 [65536, 1280], P('col', 'row'), may hold values from -0.0625 to 0.0625
Outputs:
- residual_out: bfloat16 [8192, 65536], P('row', 'col')
All inputs are finite; a program needn't handle non-finite values.
Results may differ from a plain program's by a relative error of at most 0.004.
Values may be sent and summed in bfloat16 or wider, within the bound.
A program may use at most 64 MiB of HBM per device.

v0:
```python
import jax
import jax.numpy as jnp
from jax import lax
from jax.sharding import PartitionSpec as P


def project_back(chi_block, vectors):
    return lax.dot_general(
        chi_block, vectors, (((1,), (1,)), ((), ())), preferred_element_type=jnp.float32
    )


def body(amplitudes, residual_in, cholesky):
    full_panel = lax.all_gather(cholesky, "row", axis=1, tiled=True)
    partial_value = jnp.dot(amplitudes, full_panel, preferred_element_type=jnp.float32)
    chi = lax.psum(partial_value, "col").astype(jnp.bfloat16)
    update = project_back(chi, full_panel)
    return (residual_in.astype(jnp.float32) + update).astype(jnp.bfloat16)


def solution(mesh):
    in_specs = (P("row", "col"), P("row", "col"), P("col", "row"))
    out_specs = P("row", "col")
    return jax.shard_map(body, mesh=mesh, in_specs=in_specs, out_specs=out_specs, check_vma=False)
```

profile of v0, /device:TPU:1, one launch (start us, length us, event | category | flops | bytes accessed | tf_op | source)
XLA Modules:
  0.0 329.5 jit_solution(14785733260307432897)
XLA Ops:
  6.5 0.0 all-gather.2.cloned.1.call-start
  6.5 0.7 all-gather.2.cloned.1.call-update
  7.3 129.1 %all-gather.2.cloned.1.call-done = bf16[2048,1280]{0,1:T(8,128)(2,1)} async-done(((bf16[2048,160]{0,1:T(8,128)(2,1)}), bf16[2048,1280]{0,1:T(8,128)(2,1)}) %all-gather.2.cloned.1.call-update) | async-done | bytes 5242896 | tf_op jit(solution)/shard_map/all_gather | solution.py:14
  136.3 10.5 %fusion.1 = f32[1024,1280]{1,0:T(8,128)} fusion(bf16[1024,2048]{1,0:T(8,128)(2,1)} %param.3, bf16[2048,1280]{0,1:T(8,128)(2,1)} %all-gather.2.cloned.1.call-done), kind=kOutput, calls=%fused_computation.2 | convolution fusion | flops 5368709120 | bytes 14680064 | tf_op jit(solution)/shard_map/dot_general | solution.py:15
  146.9 165.5 %all-reduce.1 = bf16[1024,1280]{1,0:T(8,128)(2,1)S(1)} all-reduce(f32[1024,1280]{1,0:T(8,128)} %fusion.1), channel_id=1, replica_groups=mesh['row'=8,'col'=32] {'col'}, use_global_device_ids=true, to_apply=%region_0.0 | all-reduce | flops 1310720 | bytes 7864320 | tf_op jit(solution)/shard_map/psum | solution.py:16
  312.4 10.2 %add_convert_fusion = bf16[1024,2048]{1,0:T(8,128)(2,1)} fusion(bf16[1024,2048]{1,0:T(8,128)(2,1)} %param.4, bf16[2048,1280]{0,1:T(8,128)(2,1)} %all-gather.2.cloned.1.call-done, bf16[1024,1280]{1,0:T(8,128)(2,1)S(1)} %all-reduce.1), kind=kOutput, calls=%fused_computation | convolution fusion | flops 5375000576 | bytes 16252928 | tf_op jit(solution)/shard_map/dot_general | solution.py:8
Async XLA Ops:
  6.5 129.8 %all-gather.2.cloned.1.call-start = ((), (), s32[]{:S(2)}) async-start(), calls=%async_computation | async-start | bytes 5898240 | tf_op jit(solution)/shard_map/all_gather | solution.py:14
Sparse Core Ops, SparseCore 0:
  10.0 126.3 all-gather.1
where the time goes:
time: 331 us; the launch traced here: 329 us
  blocking collectives  166 us (50%)
  waiting for transfers between devices  130 us (39%)
  matrix products  20.8 us (6%)
  between operations  13.4 us (4%)
    psum x1, blocking collectives, body(): chi = lax.psum(partial_value, 'col').astype(jnp.bfloat16)  166 us
    all_gather x1, waiting for transfers between devices, body(): full_panel = lax.all_gather(cholesky, 'row', axis=1, tiled=True)  129 us
    dot_general x1, matrix products, body(): jnp.dot(amplitudes, full_panel, preferred_element_type=jnp.float32)  10.5 us
    dot_general x1, matrix products, project_back(): lax.dot_general(chi_block, vectors, (((1,), (1,)), ((), ())), preferred_e...  10.2 us
  transfers between devices with their start and end apart: 1, of which 1 were waited for; matrix products, arithmetic and copies ran while one was open for 0% of the time, Pallas kernels for 0%

commit v1 on v0

v1 whole, which is shorter than its diff:
```python
import functools

import jax
import jax.numpy as jnp
from jax import lax
from jax.experimental import pallas as pl
from jax.experimental.pallas import tpu as pltpu
from jax.sharding import PartitionSpec as P

MESH = pl.DeviceIdType.MESH
BF16, F32 = jnp.bfloat16, jnp.float32

ROWS, COLS, VEC = 1024, 2048, 1280
SHARD = 160
SUBS, SUB = 5, 32
LANES = 128

ARRIVAL = (
    [(0, 0), (0, 1), (0, 2), (0, 3)]
    + [(0, 4), (1, 0), (2, 4), (1, 1), (2, 3), (1, 2), (2, 2), (1, 3), (2, 1), (1, 4), (2, 0), (4, 0)]
    + [(3, 0), (3, 4), (4, 1), (3, 1), (3, 3), (5, 0), (6, 0), (4, 2), (3, 2), (4, 3)]
    + [(5, 1), (6, 1), (5, 2), (6, 2), (4, 4), (7, 0), (5, 3), (6, 3)]
    + [(7, 1), (7, 2), (7, 3), (5, 4), (6, 4), (7, 4)]
)
PLACE = {piece: i * SUB for i, piece in enumerate(ARRIVAL)}
CHUNKS = ((4, False), (12, False), (10, False), (8, False), (6, True))
STARTS = [sum(n for n, _ in CHUNKS[:i]) for i in range(len(CHUNKS))]
GROUPS = ((0, 1), (2,), (3,), (4,))
ON_RIGHT = {1: (0, 1, 2), 5: (0, 1)}


def first_row(chunk):
    return STARTS[chunk] * SUB


def height(chunk):
    return CHUNKS[chunk][0] * SUB


def body(
    a_hbm, r_hbm, c_hbm, o_hbm,
    a, res, cv, panel, acc, chi, chit, own, sib_out, sib_in, y_out, y_in, y_sum, z_out, z_in,
    local_sem, out_sem, zx_s, zx_r, x_s, x_r, f_s, f_r, core_s, core_r, y_s, y_r, z_s, z_r, zg_s, zg_r, g_s, g_r, t_s,
):
    row, col = lax.axis_index("row"), lax.axis_index("col")
    y, zl, core = col // 8, lax.rem(col // 2, 4), lax.rem(col, 2)
    other = 1 - core

    def at(y, zl, core):
        return (row, (y * 4 + zl) * 2 + core)

    right, left = (lax.rem(row + 2, 8), col), (lax.rem(row + 6, 8), col)
    across = (row + 1 - 2 * lax.rem(row, 2), col)
    sibling = at(y, zl, other)
    ys = [lax.rem(y + d, 4) for d in range(4)]
    ys_back = [lax.rem(y + 4 - d, 4) for d in range(4)]
    zs = [lax.rem(zl + e, 4) for e in range(4)]
    partners = [right, left, across, sibling]
    partners += [at(ys[d], zl, core) for d in (1, 2, 3)]
    partners += [at(ys[d], zl, other) for d in (1, 2, 3)]
    partners += [at(y, zs[e], core) for e in (1, 2, 3)]

    barrier = pltpu.get_barrier_semaphore()
    for device in partners:
        pl.semaphore_signal(barrier, inc=1, device_id=device, device_id_type=MESH)
    load_c = pltpu.make_async_copy(c_hbm, cv, local_sem.at[0])
    load_a = pltpu.make_async_copy(a_hbm, a, local_sem.at[1])
    load_r = pltpu.make_async_copy(r_hbm, res, local_sem.at[2])
    load_c.start()
    load_a.start()
    load_r.start()
    load_c.wait()
    for piece in range(4):
        s = pl.ds(piece * 512, 512)
        turned = cv[s, :].T
        for j in range(SUBS):
            panel[pl.ds(PLACE[0, j], SUB), s] = turned[j * SUB : (j + 1) * SUB, :]
    pl.semaphore_wait(barrier, len(partners))

    unsent = []

    def send(src, dst, send_sem, recv_sem, device):
        copy = pltpu.make_async_remote_copy(
            src_ref=src, dst_ref=dst, send_sem=send_sem, recv_sem=recv_sem, device_id=device, device_id_type=MESH
        )
        copy.start()
        unsent.append(copy)
        return copy

    arriving = {}

    def move(piece, to, send_sem, recv_sem, device):
        arriving[to] = send(
            panel.at[pl.ds(PLACE[piece], SUB), :], panel.at[pl.ds(PLACE[to], SUB), :], send_sem, recv_sem, device
        )

    def need(piece):
        if piece in arriving:
            arriving.pop(piece).wait_recv()

    def both_ways(block, j, jl):
        which = block // 4
        move((block, j), (block + 1, j), x_s.at[which, 0, j], x_r.at[which, 0, j], right)
        move((block, jl), (block + 2, jl), x_s.at[which, 1, jl], x_r.at[which, 1, jl], left)

    def pass_on(block, j):
        need((block, j))
        base = 1 if block < 4 else 5
        goes_right = j in ON_RIGHT[base]
        if goes_right == (block == base):
            device = right if goes_right else left
            move((block, j), (base + 2, j), f_s.at[base // 4, j], f_r.at[base // 4, j], device)

    def from_across(j):
        need((4, j))
        both_ways(4, j, j)

    def multiply(c):
        n, direct = CHUNKS[c]
        for piece in ARRIVAL[STARTS[c] : STARTS[c] + n]:
            need(piece)
        rows = pl.ds(first_row(c), height(c))

        def half(which, into):
            for t in range(2):
                s = pl.ds(pl.multiple_of(which * 512 + t * 256, 256), 256)
                part = lax.dot_general(panel[rows, :], a[s, :], (((1,), (1,)), ((), ())), preferred_element_type=F32)
                for u in range(2):
                    tile = part[:, u * LANES : (u + 1) * LANES]
                    into[2 * t + u, rows, :] = tile
                    if direct:
                        y_out[which * 4 + 2 * t + u, rows, :] = tile.astype(BF16)

        half(other, sib_out)
        if direct:
            for d in (2, 1, 3, 0):
                send(
                    y_out.at[other * 4 + ys[d], rows, :], y_in.at[4 + d, rows, :],
                    y_s.at[c, 4 + d], y_r.at[c, 4 + d], at(ys[d], zl, other),
                )
        else:
            core_copies[c] = send(sib_out.at[:, rows, :], sib_in.at[:, rows, :], core_s.at[c], core_r.at[c], sibling)
        half(core, own)
        if direct:
            for d in (2, 1, 3):
                send_y(c, rows, d)

    core_copies = {}

    def recv(dst, sem):
        return pltpu.make_async_remote_copy(
            src_ref=dst, dst_ref=dst, send_sem=sem, recv_sem=sem, device_id=sibling, device_id_type=MESH
        )

    def send_y(c, rows, d):
        send(
            y_out.at[core * 4 + ys[d], rows, :], y_in.at[d, rows, :],
            y_s.at[c, d], y_r.at[c, d], at(ys[d], zl, core),
        )

    def scatter_y(c):
        if CHUNKS[c][1]:
            return
        rows = pl.ds(first_row(c), height(c))
        core_copies[c].wait_recv()
        for d in (2, 1, 3, 0):
            total = own[ys[d], rows, :] + sib_in[ys[d], rows, :]
            if d:
                y_out[core * 4 + ys[d], rows, :] = total.astype(BF16)
                send_y(c, rows, d)
            else:
                own[y, rows, :] = total

    def scatter_z(c):
        rows = pl.ds(first_row(c), height(c))
        part = height(c) // 4
        total = own[y, rows, :]
        for d in (1, 3, 2, 4, 5, 7, 6) if CHUNKS[c][1] else (1, 3, 2):
            recv(y_in.at[d, rows, :], y_r.at[c, d]).wait_recv()
            total = total + y_in[d, rows, :].astype(F32)
        y_sum[rows, :] = total
        z_out[rows, :] = total.astype(BF16)
        for e in (3, 2, 1):
            src = pl.ds(pl.multiple_of(first_row(c) + part * zs[e], 16), part)
            dst = pl.ds(first_row(c) // 4, part)
            send(z_out.at[src, :], z_in.at[e, dst, :], z_s.at[c, e], z_r.at[c, e], at(y, zs[e], core))

    def gather_z(c):
        part = height(c) // 4
        mine = pl.ds(pl.multiple_of(first_row(c) + part * zl, 16), part)
        total = y_sum[mine, :]
        for e in (1, 2, 3):
            slot = pl.ds(first_row(c) // 4, part)
            recv(z_in.at[e, slot, :], z_r.at[c, e]).wait_recv()
            total = total + z_in[e, slot, :].astype(F32)
        tile = core * 4 + y
        chi[tile, mine, :] = total.astype(BF16)
        for e in (3, 2, 1):
            piece = chi.at[tile, mine, :]
            send(piece, piece, zg_s.at[c, e], zg_r.at[c, e], at(y, zs[e], core))

    def gather_y(c):
        rows = pl.ds(first_row(c), height(c))
        part = height(c) // 4
        tile = chi.at[core * 4 + y, rows, :]
        for e in (1, 2, 3):
            theirs = pl.ds(pl.multiple_of(first_row(c) + part * lax.rem(zl + 4 - e, 4), 16), part)
            recv(chi.at[core * 4 + y, theirs, :], zg_r.at[c, e]).wait_recv()
        for d in (2, 1, 3):
            send(tile, tile, g_s.at[c, d], g_r.at[c, d], at(ys[d], zl, core))
            if CHUNKS[c][1]:
                send(tile, tile, g_s.at[c, 4 + d], g_r.at[c, 4 + d], at(ys[d], zl, other))
        send(tile, tile, g_s.at[c, 4], g_r.at[c, 4], sibling)

    def gather_core(c):
        rows = pl.ds(first_row(c), height(c))
        for d in (1, 3, 2):
            tile = chi.at[core * 4 + ys_back[d], rows, :]
            recv(tile, g_r.at[c, d]).wait_recv()
            if not CHUNKS[c][1]:
                send(tile, tile, g_s.at[c, 4 + d], g_r.at[c, 4 + d], sibling)

    def multiply_back(g):
        group = GROUPS[g]
        for c in group:
            for d in (0, 1, 3, 2):
                tile = chi.at[other * 4 + ys_back[d], pl.ds(first_row(c), height(c)), :]
                recv(tile, g_r.at[c, 4 + d]).wait_recv()
        rows = pl.ds(first_row(group[0]), sum(height(c) for c in group))
        depth = sum(height(c) for c in group)
        for t in range(8):
            chit[pl.ds(t * LANES, LANES), pl.ds(0, depth)] = chi[t, rows, :].T
        last = g == len(GROUPS) - 1

        @pl.loop(0, COLS // 256)
        def _(i):
            s = pl.ds(pl.multiple_of(i * 256, 256), 256)
            update = jnp.dot(chit[:, pl.ds(0, depth)], panel[rows, s], preferred_element_type=F32)
            if last:
                res[:, s] = (res[:, s].astype(F32) + (acc[:, s] + update)).astype(BF16)
                pltpu.make_async_copy(res.at[:, s], o_hbm.at[:, s], out_sem.at[i]).start()
            elif g == 0:
                acc[:, s] = update
            else:
                acc[:, s] += update

    steps = []

    def when(time, step, *args):
        steps.append((time, len(steps), functools.partial(step, *args)))

    for j in range(SUBS):
        when(6 * (j + 1), from_across, j)
        when(3 * (j + 1), pass_on, 1, j)
        when(3 * (j + 1), pass_on, 2, SUBS - 1 - j)
        when((23, 29, 32, 36, 39)[j], pass_on, 5, j)
        when((23, 29, 32, 36, 39)[j], pass_on, 6, j)
    ready = (0.5, 16, 26, 36, 43)
    for c, start in enumerate(ready):
        for delay, step in enumerate((multiply, scatter_y, scatter_z, gather_z, gather_y, gather_core)):
            when(start + (0, 3, 6, 9, 12, 15)[delay], step, c)
    for g, group in enumerate(GROUPS):
        when(ready[group[-1]] + 17, multiply_back, g)

    for j in range(SUBS):
        move((0, j), (4, j), zx_s.at[j], zx_r.at[j], across)
    for j in range(SUBS):
        both_ways(0, j, SUBS - 1 - j)
    load_a.wait()
    load_r.wait()
    for _, _, step in sorted(steps, key=lambda s: s[:2]):
        step()
    for copy in unsent:
        copy.wait_send()
    for i in range(COLS // 256):
        s = pl.ds(i * 256, 256)
        pltpu.make_async_copy(res.at[:, s], o_hbm.at[:, s], out_sem.at[i]).wait()


def cycle_term(amplitudes, residual_in, cholesky):
    dma = pltpu.SemaphoreType.DMA
    n = len(CHUNKS)
    depth = max(sum(height(c) for c in g) for g in GROUPS)
    any_space = pl.BlockSpec(memory_space=pl.ANY)
    return pl.pallas_call(
        body,
        name="cycle_term",
        out_shape=jax.ShapeDtypeStruct((ROWS, COLS), BF16),
        in_specs=[any_space] * 3,
        out_specs=any_space,
        scratch_shapes=[
            pltpu.VMEM((ROWS, COLS), BF16),
            pltpu.VMEM((ROWS, COLS), BF16),
            pltpu.VMEM((COLS, SHARD), BF16),
            pltpu.VMEM((VEC, COLS), BF16),
            pltpu.VMEM((ROWS, COLS), F32),
            pltpu.VMEM((8, VEC, LANES), BF16),
            pltpu.VMEM((ROWS, depth), BF16),
            pltpu.VMEM((4, VEC, LANES), F32),
            pltpu.VMEM((4, VEC, LANES), F32),
            pltpu.VMEM((4, VEC, LANES), F32),
            pltpu.VMEM((8, VEC, LANES), BF16),
            pltpu.VMEM((8, VEC, LANES), BF16),
            pltpu.VMEM((VEC, LANES), F32),
            pltpu.VMEM((VEC, LANES), BF16),
            pltpu.VMEM((4, VEC // 4, LANES), BF16),
            dma((3,)), dma((COLS // 256,)),
            dma((SUBS,)), dma((SUBS,)),
            dma((2, 2, SUBS)), dma((2, 2, SUBS)),
            dma((2, SUBS)), dma((2, SUBS)),
            dma((n,)), dma((n,)),
            dma((n, 8)), dma((n, 8)),
            dma((n, 4)), dma((n, 4)),
            dma((n, 4)), dma((n, 4)),
            dma((n, 8)), dma((n, 8)),
            dma((1,)),
        ],
        compiler_params=pltpu.CompilerParams(collective_id=0, has_side_effects=True, vmem_limit_bytes=56 << 20),
        cost_estimate=pl.CostEstimate(flops=4 * ROWS * COLS * VEC, bytes_accessed=14 << 20, transcendentals=0),
    )(amplitudes, residual_in, cholesky)


def solution(mesh):
    in_specs = (P("row", "col"), P("row", "col"), P("col", "row"))
    out_specs = P("row", "col")
    return jax.shard_map(cycle_term, mesh=mesh, in_specs=in_specs, out_specs=out_specs, check_vma=False)
```

time: 331 us -> 126 us (0.38)
  blocking collectives: 166 us -> 0 us
  waiting for transfers between devices: 130 us -> 0 us
  Pallas kernels: 0 us -> 119 us
  matrix products: 20.8 us -> 0 us
  between operations: 13.4 us -> 0.01 us
  local copies, waits for them, and re-layouts: 0 us -> 6.98 us
    psum x1 -> x0, blocking collectives: 166 us -> none  [body(): chi = lax.psum(partial_value, 'col').astype(jnp.bfloat16)]
    all_gather x1 -> x0, waiting for transfers between devices: 129 us -> none  [body(): full_panel = lax.all_gather(cholesky, 'row', axis=1, tiled=True)]
    pallas_call x0 -> x1, Pallas kernels: none -> 119 us  [cycle_term(): pl.pallas_call(body, name='cycle_term', out_shape=jax.ShapeDtypeStruct((R...]
    dot_general x2 -> x0, matrix products: 20.8 us -> none  [the longest x1 10.5 us: body(): jnp.dot(amplitudes, full_panel, preferred_element_type=jnp.float32)]
    unnamed x0 -> x2, local copies, waits for them, and re-layouts: none -> 6.98 us
  transfers between devices with their start and end apart: 1 -> 0, of which waited for: 1 -> 0; matrix products, arithmetic and copies ran while one was open for 0% -> 0% of each run, Pallas kernels for 0% -> 0%
where the time goes in v1:
time: 126 us
  Pallas kernels  119 us (94%)
  local copies, waits for them, and re-layouts  6.98 us (6%)
    pallas_call x1, Pallas kernels, cycle_term(): pl.pallas_call(body, name='cycle_term', out_shape=jax.ShapeDtypeStruct((R...  119 us
    unnamed x2, local copies, waits for them, and re-layouts  6.98 us

profile of v1, /device:TPU:1, one launch (start us, length us, event | category | flops | bytes accessed | tf_op | source)
XLA Modules:
  0.0 125.8 jit_solution(4338071400306579902)
XLA Ops:
  0.0 2.2 %copy.4.c_hbm = bf16[2048,160]{1,0:T(8,128)(2,1)} copy(bf16[2048,160]{0,1:T(8,128)(2,1)} %param.5) | data formatting | bytes 1310720 | tf_op args[2]
  2.2 118.8 %cycle_term.1 = bf16[1024,2048]{1,0:T(8,128)(2,1)} custom-call(bf16[1024,2048]{1,0:T(8,128)(2,1)} %a_hbm.1, bf16[1024,2048]{1,0:T(8,128)(2,1)} %r_hbm.1, bf16[2048,160]{1,0:T(8,128)(2,1)} %copy.4.c_hbm), custom_call_target="tpu_custom_call" | custom-call | flops 10737418240 | bytes 14680064 | tf_op jit(solution)/shard_map/cycle_term/pallas_call | solution.py:285
  121.0 4.8 %copy.6 = bf16[1024,2048]{1,0:T(8,128)(2,1)} copy(bf16[1024,2048]{1,0:T(8,128)(2,1)} %cycle_term.1) | data formatting | bytes 8388608

commit v2 on v1

--- a/solution.py
+++ b/solution.py
@@ -16,16 +16,23 @@
 LANES = 128
 
 ARRIVAL = (
-    [(0, 0), (0, 1), (0, 2), (0, 3)]
-    + [(0, 4), (1, 0), (2, 4), (1, 1), (2, 3), (1, 2), (2, 2), (1, 3), (2, 1), (1, 4), (2, 0), (4, 0)]
-    + [(3, 0), (3, 4), (4, 1), (3, 1), (3, 3), (5, 0), (6, 0), (4, 2), (3, 2), (4, 3)]
-    + [(5, 1), (6, 1), (5, 2), (6, 2), (4, 4), (7, 0), (5, 3), (6, 3)]
-    + [(7, 1), (7, 2), (7, 3), (5, 4), (6, 4), (7, 4)]
+    [(0, 0), (0, 1), (0, 2), (0, 3), (0, 4), (1, 0), (2, 4), (1, 1)]
+    + [(2, 3), (1, 2), (2, 2), (1, 3), (2, 1), (1, 4), (2, 0), (4, 0)]
+    + [(4, 1), (3, 0), (3, 4), (3, 1), (4, 2), (5, 0), (6, 0), (3, 3)]
+    + [(3, 2), (4, 3), (5, 1), (6, 1), (5, 2), (6, 2), (6, 3), (4, 4)]
+    + [(7, 0), (7, 2), (5, 3), (6, 4)]
+    + [(7, 1), (7, 3)]
+    + [(5, 4), (7, 4)]
 )
 PLACE = {piece: i * SUB for i, piece in enumerate(ARRIVAL)}
-CHUNKS = ((4, False), (12, False), (10, False), (8, False), (6, True))
-STARTS = [sum(n for n, _ in CHUNKS[:i]) for i in range(len(CHUNKS))]
-GROUPS = ((0, 1), (2,), (3,), (4,))
+CHUNKS = (
+    (8, False, False), (8, False, False), (8, False, False), (8, False, False),
+    (4, False, True), (2, True, True), (2, True, True),
+)
+STARTS = [sum(chunk[0] for chunk in CHUNKS[:i]) for i in range(len(CHUNKS))]
+GROUPS = ((0,), (1,), (2,), (3,), (4, 5, 6))
+PARTS = 4
+SLICES, SLICE = 10, 16
 ON_RIGHT = {1: (0, 1, 2), 5: (0, 1)}
 
 
@@ -38,9 +45,9 @@
 
 
 def body(
-    a_hbm, r_hbm, c_hbm, o_hbm,
-    a, res, cv, panel, acc, chi, chit, own, sib_out, sib_in, y_out, y_in, y_sum, z_out, z_in,
-    local_sem, out_sem, zx_s, zx_r, x_s, x_r, f_s, f_r, core_s, core_r, y_s, y_r, z_s, z_r, zg_s, zg_r, g_s, g_r, t_s,
+    a_hbm, r_hbm, c_hbm, out,
+    a, res, panel, acc, chi, own, sib_out, sib_in, y_out, y_in, y_sum, z_out, z_in,
+    local_sem, own_sem, zx_s, zx_r, x_s, x_r, f_s, f_r, core_s, core_r, y_s, y_r, z_s, z_r, zg_s, zg_r, g_s, g_r,
 ):
     row, col = lax.axis_index("row"), lax.axis_index("col")
     y, zl, core = col // 8, lax.rem(col // 2, 4), lax.rem(col, 2)
@@ -63,18 +70,18 @@
     barrier = pltpu.get_barrier_semaphore()
     for device in partners:
         pl.semaphore_signal(barrier, inc=1, device_id=device, device_id_type=MESH)
-    load_c = pltpu.make_async_copy(c_hbm, cv, local_sem.at[0])
-    load_a = pltpu.make_async_copy(a_hbm, a, local_sem.at[1])
-    load_r = pltpu.make_async_copy(r_hbm, res, local_sem.at[2])
-    load_c.start()
+    load_c = [
+        pltpu.make_async_copy(c_hbm.at[pl.ds(j * SUB, SUB), :], panel.at[pl.ds(PLACE[0, j], SUB), :], own_sem.at[j])
+        for j in range(SUBS)
+    ]
+    load_a = pltpu.make_async_copy(a_hbm, a, local_sem.at[0])
+    load_r = pltpu.make_async_copy(r_hbm, res, local_sem.at[1])
+    for load in load_c:
+        load.start()
     load_a.start()
     load_r.start()
-    load_c.wait()
-    for piece in range(4):
-        s = pl.ds(piece * 512, 512)
-        turned = cv[s, :].T
-        for j in range(SUBS):
-            panel[pl.ds(PLACE[0, j], SUB), s] = turned[j * SUB : (j + 1) * SUB, :]
+    for load in load_c:
+        load.wait()
     pl.semaphore_wait(barrier, len(partners))
 
     unsent = []
@@ -98,6 +105,20 @@
         if piece in arriving:
             arriving.pop(piece).wait_recv()
 
+    crossing = []
+
+    def cross(count):
+        for i in range(len(crossing), len(crossing) + count):
+            j, offset = i * SLICE // SUB, i * SLICE % SUB
+            src, dst = (pl.ds(PLACE[block, j] + offset, SLICE) for block in (0, 4))
+            crossing.append(send(panel.at[src, :], panel.at[dst, :], zx_s.at[i], zx_r.at[i], across))
+
+    def crossed(i):
+        crossing[i].wait_recv()
+        j, offset = i * SLICE // SUB, i * SLICE % SUB
+        if offset + SLICE == SUB:
+            both_ways(4, j, j)
+
     def both_ways(block, j, jl):
         which = block // 4
         move((block, j), (block + 1, j), x_s.at[which, 0, j], x_r.at[which, 0, j], right)
@@ -111,25 +132,20 @@
             device = right if goes_right else left
             move((block, j), (base + 2, j), f_s.at[base // 4, j], f_r.at[base // 4, j], device)
 
-    def from_across(j):
-        need((4, j))
-        both_ways(4, j, j)
-
     def multiply(c):
-        n, direct = CHUNKS[c]
+        n, direct, _ = CHUNKS[c]
         for piece in ARRIVAL[STARTS[c] : STARTS[c] + n]:
             need(piece)
         rows = pl.ds(first_row(c), height(c))
 
         def half(which, into):
-            for t in range(2):
-                s = pl.ds(pl.multiple_of(which * 512 + t * 256, 256), 256)
-                part = lax.dot_general(panel[rows, :], a[s, :], (((1,), (1,)), ((), ())), preferred_element_type=F32)
-                for u in range(2):
-                    tile = part[:, u * LANES : (u + 1) * LANES]
-                    into[2 * t + u, rows, :] = tile
-                    if direct:
-                        y_out[which * 4 + 2 * t + u, rows, :] = tile.astype(BF16)
+            s = pl.ds(pl.multiple_of(which * 512, 512), 512)
+            part = lax.dot_general(panel[rows, :], a[s, :], (((1,), (1,)), ((), ())), preferred_element_type=F32)
+            for t in range(4):
+                tile = part[:, t * LANES : (t + 1) * LANES]
+                into[t, rows, :] = tile
+                if direct:
+                    y_out[which * 4 + t, rows, :] = tile.astype(BF16)
 
         half(other, sib_out)
         if direct:
@@ -180,12 +196,18 @@
             total = total + y_in[d, rows, :].astype(F32)
         y_sum[rows, :] = total
         z_out[rows, :] = total.astype(BF16)
+        if CHUNKS[c][2]:
+            for e in (3, 2, 1):
+                send(z_out.at[rows, :], z_in.at[e, rows, :], z_s.at[c, e], z_r.at[c, e], at(y, zs[e], core))
+            return
         for e in (3, 2, 1):
             src = pl.ds(pl.multiple_of(first_row(c) + part * zs[e], 16), part)
             dst = pl.ds(first_row(c) // 4, part)
             send(z_out.at[src, :], z_in.at[e, dst, :], z_s.at[c, e], z_r.at[c, e], at(y, zs[e], core))
 
     def gather_z(c):
+        if CHUNKS[c][2]:
+            return
         part = height(c) // 4
         mine = pl.ds(pl.multiple_of(first_row(c) + part * zl, 16), part)
         total = y_sum[mine, :]
@@ -203,7 +225,13 @@
         rows = pl.ds(first_row(c), height(c))
         part = height(c) // 4
         tile = chi.at[core * 4 + y, rows, :]
-        for e in (1, 2, 3):
+        if CHUNKS[c][2]:
+            total = y_sum[rows, :]
+            for e in (1, 2, 3):
+                recv(z_in.at[e, rows, :], z_r.at[c, e]).wait_recv()
+                total = total + z_in[e, rows, :].astype(F32)
+            chi[core * 4 + y, rows, :] = total.astype(BF16)
+        for e in () if CHUNKS[c][2] else (1, 2, 3):
             theirs = pl.ds(pl.multiple_of(first_row(c) + part * lax.rem(zl + 4 - e, 4), 16), part)
             recv(chi.at[core * 4 + y, theirs, :], zg_r.at[c, e]).wait_recv()
         for d in (2, 1, 3):
@@ -220,50 +248,58 @@
             if not CHUNKS[c][1]:
                 send(tile, tile, g_s.at[c, 4 + d], g_r.at[c, 4 + d], sibling)
 
-    def multiply_back(g):
+    def multiply_back(g, part):
         group = GROUPS[g]
-        for c in group:
-            for d in (0, 1, 3, 2):
-                tile = chi.at[other * 4 + ys_back[d], pl.ds(first_row(c), height(c)), :]
-                recv(tile, g_r.at[c, 4 + d]).wait_recv()
-        rows = pl.ds(first_row(group[0]), sum(height(c) for c in group))
         depth = sum(height(c) for c in group)
-        for t in range(8):
-            chit[pl.ds(t * LANES, LANES), pl.ds(0, depth)] = chi[t, rows, :].T
-        last = g == len(GROUPS) - 1
-
-        @pl.loop(0, COLS // 256)
-        def _(i):
-            s = pl.ds(pl.multiple_of(i * 256, 256), 256)
-            update = jnp.dot(chit[:, pl.ds(0, depth)], panel[rows, s], preferred_element_type=F32)
-            if last:
-                res[:, s] = (res[:, s].astype(F32) + (acc[:, s] + update)).astype(BF16)
-                pltpu.make_async_copy(res.at[:, s], o_hbm.at[:, s], out_sem.at[i]).start()
+        rows = pl.ds(first_row(group[0]), depth)
+        if part == 0:
+            for c in group:
+                for d in (0, 1, 3, 2):
+                    tile = chi.at[other * 4 + ys_back[d], pl.ds(first_row(c), height(c)), :]
+                    recv(tile, g_r.at[c, 4 + d]).wait_recv()
+        for t in range(part * 8 // PARTS, (part + 1) * 8 // PARTS):
+            s = pl.ds(t * LANES, LANES)
+            update = jnp.dot(chi[t, rows, :].T, panel[rows, :], preferred_element_type=F32)
+            if g == len(GROUPS) - 1:
+                out[s, :] = (res[s, :].astype(F32) + (acc[s, :] + update)).astype(BF16)
             elif g == 0:
-                acc[:, s] = update
+                acc[s, :] = update
             else:
-                acc[:, s] += update
+                acc[s, :] += update
 
     steps = []
 
     def when(time, step, *args):
         steps.append((time, len(steps), functools.partial(step, *args)))
 
-    for j in range(SUBS):
-        when(6 * (j + 1), from_across, j)
-        when(3 * (j + 1), pass_on, 1, j)
-        when(3 * (j + 1), pass_on, 2, SUBS - 1 - j)
-        when((23, 29, 32, 36, 39)[j], pass_on, 5, j)
-        when((23, 29, 32, 36, 39)[j], pass_on, 6, j)
-    ready = (0.5, 16, 26, 36, 43)
-    for c, start in enumerate(ready):
-        for delay, step in enumerate((multiply, scatter_y, scatter_z, gather_z, gather_y, gather_core)):
-            when(start + (0, 3, 6, 9, 12, 15)[delay], step, c)
-    for g, group in enumerate(GROUPS):
-        when(ready[group[-1]] + 17, multiply_back, g)
-
-    for j in range(SUBS):
-        move((0, j), (4, j), zx_s.at[j], zx_r.at[j], across)
+    for i, time in enumerate((7.2, 10.3, 12.8, 15.9, 19.4, 21.5, 25, 28, 30.8, 33.5)):
+        when(time, crossed, i)
+    for j, time in enumerate((5.6, 8.6, 11.8, 14.5, 17.4)):
+        for block in (1, 2):
+            k = j if block == 1 else SUBS - 1 - j
+            if (k in ON_RIGHT[1]) == (block == 1):
+                when(time, pass_on, block, k)
+    for time, block, j in ((26.1, 5, 0), (32.2, 5, 1), (32.7, 6, 2), (34.8, 6, 3), (41.5, 6, 4)):
+        when(time, pass_on, block, j)
+    plan = (
+        (8.7, 13.3, 19.5, 30.7, 36.5, 43.2),
+        (17.5, 22, 33.6, 38.4, 43.3, 50),
+        (26.2, 30.9, 37, 43.4, 47.2, 53.5),
+        (34.9, 38.9, 44, 47.3, 51.2, 57),
+        (41.6, 45.1, 49.8, 0, 54.5, 58.5),
+        (44.1, 0, 50.1, 0, 54.7, 59),
+        (45.5, 0, 51, 0, 55.1, 59.1),
+    )
+    for c, times in enumerate(plan):
+        for time, step in zip(times, (multiply, scatter_y, scatter_z, gather_z, gather_y, gather_core), strict=True):
+            if time:
+                when(time, step, c)
+    when(19.6, cross, 3)
+    for g, times in enumerate(((47.4, 47.5, 49, 49.1), (51.1, 51.3, 52, 53), (55.2, 55.3, 55.4, 55.5), (58.6,) * 4, (60,) * 4)):
+        for part, time in enumerate(times):
+            when(time, multiply_back, g, part)
+
+    cross(7)
     for j in range(SUBS):
         both_ways(0, j, SUBS - 1 - j)
     load_a.wait()
@@ -272,30 +308,24 @@
         step()
     for copy in unsent:
         copy.wait_send()
-    for i in range(COLS // 256):
-        s = pl.ds(i * 256, 256)
-        pltpu.make_async_copy(res.at[:, s], o_hbm.at[:, s], out_sem.at[i]).wait()
 
 
 def cycle_term(amplitudes, residual_in, cholesky):
     dma = pltpu.SemaphoreType.DMA
     n = len(CHUNKS)
-    depth = max(sum(height(c) for c in g) for g in GROUPS)
     any_space = pl.BlockSpec(memory_space=pl.ANY)
     return pl.pallas_call(
         body,
         name="cycle_term",
-        out_shape=jax.ShapeDtypeStruct((ROWS, COLS), BF16),
+        out_shape=pltpu.VMEM((ROWS, COLS), BF16),
         in_specs=[any_space] * 3,
-        out_specs=any_space,
+        out_specs=pl.BlockSpec(memory_space=pltpu.VMEM),
         scratch_shapes=[
             pltpu.VMEM((ROWS, COLS), BF16),
             pltpu.VMEM((ROWS, COLS), BF16),
-            pltpu.VMEM((COLS, SHARD), BF16),
             pltpu.VMEM((VEC, COLS), BF16),
             pltpu.VMEM((ROWS, COLS), F32),
             pltpu.VMEM((8, VEC, LANES), BF16),
-            pltpu.VMEM((ROWS, depth), BF16),
             pltpu.VMEM((4, VEC, LANES), F32),
             pltpu.VMEM((4, VEC, LANES), F32),
             pltpu.VMEM((4, VEC, LANES), F32),
@@ -303,9 +333,9 @@
             pltpu.VMEM((8, VEC, LANES), BF16),
             pltpu.VMEM((VEC, LANES), F32),
             pltpu.VMEM((VEC, LANES), BF16),
-            pltpu.VMEM((4, VEC // 4, LANES), BF16),
-            dma((3,)), dma((COLS // 256,)),
-            dma((SUBS,)), dma((SUBS,)),
+            pltpu.VMEM((4, VEC, LANES), BF16),
+            dma((2,)), dma((SUBS,)),
+            dma((SLICES,)), dma((SLICES,)),
             dma((2, 2, SUBS)), dma((2, 2, SUBS)),
             dma((2, SUBS)), dma((2, SUBS)),
             dma((n,)), dma((n,)),
@@ -313,11 +343,10 @@
             dma((n, 4)), dma((n, 4)),
             dma((n, 4)), dma((n, 4)),
             dma((n, 8)), dma((n, 8)),
-            dma((1,)),
         ],
-        compiler_params=pltpu.CompilerParams(collective_id=0, has_side_effects=True, vmem_limit_bytes=56 << 20),
+        compiler_params=pltpu.CompilerParams(collective_id=0, has_side_effects=True, vmem_limit_bytes=58 << 20),
         cost_estimate=pl.CostEstimate(flops=4 * ROWS * COLS * VEC, bytes_accessed=14 << 20, transcendentals=0),
-    )(amplitudes, residual_in, cholesky)
+    )(amplitudes, residual_in, cholesky.T)
 
 
 def solution(mesh):

time: 126 us -> 81 us (0.64)
  Pallas kernels: 119 us -> 78.8 us
  local copies, waits for them, and re-layouts: 6.98 us -> 2.02 us
    pallas_call x1, Pallas kernels: 119 us -> 78.8 us  [cycle_term(): pl.pallas_call(body, name='cycle_term', out_shape=pltpu.VMEM((ROWS, COLS)...]
    unnamed x2 -> x1, local copies, waits for them, and re-layouts: 6.98 us -> 2.02 us
where the time goes in v2:
time: 81 us; the launch traced here: 80.8 us
  Pallas kernels  78.8 us (97%)
  local copies, waits for them, and re-layouts  2.02 us (2%)
    pallas_call x1, Pallas kernels, cycle_term(): pl.pallas_call(body, name='cycle_term', out_shape=pltpu.VMEM((ROWS, COLS)...  78.8 us
    unnamed x1, local copies, waits for them, and re-layouts  2.02 us

profile of v2, /device:TPU:1, one launch (start us, length us, event | category | flops | bytes accessed | tf_op | source)
XLA Modules:
  0.0 80.8 jit_solution(17117737739605122907)
XLA Ops:
  0.0 78.8 %cycle_term.1 = bf16[1024,2048]{1,0:T(8,128)(2,1)S(1)} custom-call(bf16[1024,2048]{1,0:T(8,128)(2,1)} %a_hbm.1, bf16[1024,2048]{1,0:T(8,128)(2,1)} %r_hbm.1, bf16[160,2048]{1,0:T(8,128)(2,1)} %bitcast.1), custom_call_target="tpu_custom_call" | custom-call | flops 10737418240 | bytes 14680064 | tf_op jit(solution)/shard_map/cycle_term/pallas_call | solution.py:317
  78.8 2.0 %copy.5 = bf16[1024,2048]{1,0:T(8,128)(2,1)} copy(bf16[1024,2048]{1,0:T(8,128)(2,1)S(1)} %cycle_term.1) | data formatting | bytes 8388608

commit v3 on v2

--- a/solution.py
+++ b/solution.py
@@ -26,11 +26,18 @@
 )
 PLACE = {piece: i * SUB for i, piece in enumerate(ARRIVAL)}
 CHUNKS = (
-    (8, False, False), (8, False, False), (8, False, False), (8, False, False),
-    (4, False, True), (2, True, True), (2, True, True),
+    (8, False, False, False),
+    (8, False, False, False),
+    (8, False, False, False),
+    (4, False, False, False),
+    (4, True, False, False),
+    (2, False, True, False),
+    (2, False, True, False),
+    (2, False, True, False),
+    (2, True, True, True),
 )
 STARTS = [sum(chunk[0] for chunk in CHUNKS[:i]) for i in range(len(CHUNKS))]
-GROUPS = ((0,), (1,), (2,), (3,), (4, 5, 6))
+GROUPS = ((0,), (1,), (2,), (3, 4), (5, 6, 7, 8))
 PARTS = 4
 SLICES, SLICE = 10, 16
 ON_RIGHT = {1: (0, 1, 2), 5: (0, 1)}
@@ -46,7 +53,7 @@
 
 def body(
     a_hbm, r_hbm, c_hbm, out,
-    a, res, panel, acc, chi, own, sib_out, sib_in, y_out, y_in, y_sum, z_out, z_in,
+    a, a_turned, res, panel, acc, chi, own, sib_out, sib_in, y_out, y_in, y_sum, z_out, z_in,
     local_sem, own_sem, zx_s, zx_r, x_s, x_r, f_s, f_r, core_s, core_r, y_s, y_r, z_s, z_r, zg_s, zg_r, g_s, g_r,
 ):
     row, col = lax.axis_index("row"), lax.axis_index("col")
@@ -62,10 +69,11 @@
     ys = [lax.rem(y + d, 4) for d in range(4)]
     ys_back = [lax.rem(y + 4 - d, 4) for d in range(4)]
     zs = [lax.rem(zl + e, 4) for e in range(4)]
-    partners = [right, left, across, sibling]
+    partners = [across, right, left]
     partners += [at(ys[d], zl, core) for d in (1, 2, 3)]
     partners += [at(ys[d], zl, other) for d in (1, 2, 3)]
     partners += [at(y, zs[e], core) for e in (1, 2, 3)]
+    partners += [sibling]
 
     barrier = pltpu.get_barrier_semaphore()
     for device in partners:
@@ -80,8 +88,6 @@
         load.start()
     load_a.start()
     load_r.start()
-    for load in load_c:
-        load.wait()
     pl.semaphore_wait(barrier, len(partners))
 
     unsent = []
@@ -97,8 +103,10 @@
     arriving = {}
 
     def move(piece, to, send_sem, recv_sem, device):
+        block, j = piece
+        src = panel.at[pl.ds(PLACE[piece], SUB), :] if block else c_hbm.at[pl.ds(j * SUB, SUB), :]
         arriving[to] = send(
-            panel.at[pl.ds(PLACE[piece], SUB), :], panel.at[pl.ds(PLACE[to], SUB), :], send_sem, recv_sem, device
+            src, panel.at[pl.ds(PLACE[to], SUB), :], send_sem, recv_sem, device
         )
 
     def need(piece):
@@ -110,8 +118,8 @@
     def cross(count):
         for i in range(len(crossing), len(crossing) + count):
             j, offset = i * SLICE // SUB, i * SLICE % SUB
-            src, dst = (pl.ds(PLACE[block, j] + offset, SLICE) for block in (0, 4))
-            crossing.append(send(panel.at[src, :], panel.at[dst, :], zx_s.at[i], zx_r.at[i], across))
+            src, dst = pl.ds(i * SLICE, SLICE), pl.ds(PLACE[4, j] + offset, SLICE)
+            crossing.append(send(c_hbm.at[src, :], panel.at[dst, :], zx_s.at[i], zx_r.at[i], across))
 
     def crossed(i):
         crossing[i].wait_recv()
@@ -133,14 +141,14 @@
             move((block, j), (base + 2, j), f_s.at[base // 4, j], f_r.at[base // 4, j], device)
 
     def multiply(c):
-        n, direct, _ = CHUNKS[c]
+        n, direct, _, _ = CHUNKS[c]
         for piece in ARRIVAL[STARTS[c] : STARTS[c] + n]:
             need(piece)
         rows = pl.ds(first_row(c), height(c))
 
         def half(which, into):
             s = pl.ds(pl.multiple_of(which * 512, 512), 512)
-            part = lax.dot_general(panel[rows, :], a[s, :], (((1,), (1,)), ((), ())), preferred_element_type=F32)
+            part = jnp.dot(panel[rows, :], a_turned[:, s], preferred_element_type=F32)
             for t in range(4):
                 tile = part[:, t * LANES : (t + 1) * LANES]
                 into[t, rows, :] = tile
@@ -236,7 +244,7 @@
             recv(chi.at[core * 4 + y, theirs, :], zg_r.at[c, e]).wait_recv()
         for d in (2, 1, 3):
             send(tile, tile, g_s.at[c, d], g_r.at[c, d], at(ys[d], zl, core))
-            if CHUNKS[c][1]:
+            if CHUNKS[c][3]:
                 send(tile, tile, g_s.at[c, 4 + d], g_r.at[c, 4 + d], at(ys[d], zl, other))
         send(tile, tile, g_s.at[c, 4], g_r.at[c, 4], sibling)
 
@@ -245,7 +253,7 @@
         for d in (1, 3, 2):
             tile = chi.at[core * 4 + ys_back[d], rows, :]
             recv(tile, g_r.at[c, d]).wait_recv()
-            if not CHUNKS[c][1]:
+            if not CHUNKS[c][3]:
                 send(tile, tile, g_s.at[c, 4 + d], g_r.at[c, 4 + d], sibling)
 
     def multiply_back(g, part):
@@ -267,45 +275,107 @@
             else:
                 acc[s, :] += update
 
-    steps = []
-
-    def when(time, step, *args):
-        steps.append((time, len(steps), functools.partial(step, *args)))
-
-    for i, time in enumerate((7.2, 10.3, 12.8, 15.9, 19.4, 21.5, 25, 28, 30.8, 33.5)):
-        when(time, crossed, i)
-    for j, time in enumerate((5.6, 8.6, 11.8, 14.5, 17.4)):
-        for block in (1, 2):
-            k = j if block == 1 else SUBS - 1 - j
-            if (k in ON_RIGHT[1]) == (block == 1):
-                when(time, pass_on, block, k)
-    for time, block, j in ((26.1, 5, 0), (32.2, 5, 1), (32.7, 6, 2), (34.8, 6, 3), (41.5, 6, 4)):
-        when(time, pass_on, block, j)
-    plan = (
-        (8.7, 13.3, 19.5, 30.7, 36.5, 43.2),
-        (17.5, 22, 33.6, 38.4, 43.3, 50),
-        (26.2, 30.9, 37, 43.4, 47.2, 53.5),
-        (34.9, 38.9, 44, 47.3, 51.2, 57),
-        (41.6, 45.1, 49.8, 0, 54.5, 58.5),
-        (44.1, 0, 50.1, 0, 54.7, 59),
-        (45.5, 0, 51, 0, 55.1, 59.1),
-    )
-    for c, times in enumerate(plan):
-        for time, step in zip(times, (multiply, scatter_y, scatter_z, gather_z, gather_y, gather_core), strict=True):
-            if time:
-                when(time, step, c)
-    when(19.6, cross, 3)
-    for g, times in enumerate(((47.4, 47.5, 49, 49.1), (51.1, 51.3, 52, 53), (55.2, 55.3, 55.4, 55.5), (58.6,) * 4, (60,) * 4)):
-        for part, time in enumerate(times):
-            when(time, multiply_back, g, part)
-
-    cross(7)
+    cross(10)
     for j in range(SUBS):
         both_ways(0, j, SUBS - 1 - j)
+    for load in load_c:
+        load.wait()
     load_a.wait()
     load_r.wait()
-    for _, _, step in sorted(steps, key=lambda s: s[:2]):
-        step()
+
+    @pl.loop(0, ROWS // LANES)
+    def _(t):
+        s = pl.ds(pl.multiple_of(t * LANES, LANES), LANES)
+        a_turned[:, s] = a[s, :].T
+
+    pass_on(1, 0)
+    pass_on(2, 4)
+    crossed(0)
+    pass_on(1, 1)
+    pass_on(2, 3)
+    multiply(0)
+    crossed(1)
+    pass_on(1, 2)
+    scatter_y(0)
+    crossed(2)
+    crossed(3)
+    multiply(1)
+    crossed(4)
+    scatter_z(0)
+    scatter_y(1)
+    crossed(5)
+    crossed(6)
+    pass_on(5, 0)
+    multiply(2)
+    crossed(7)
+    scatter_z(1)
+    scatter_y(2)
+    crossed(8)
+    pass_on(5, 1)
+    pass_on(6, 2)
+    multiply(3)
+    crossed(9)
+    gather_z(0)
+    scatter_y(3)
+    pass_on(6, 3)
+    multiply(4)
+    scatter_z(2)
+    gather_z(1)
+    multiply(5)
+    gather_y(0)
+    scatter_z(3)
+    scatter_y(5)
+    pass_on(6, 4)
+    multiply(6)
+    gather_z(2)
+    scatter_z(4)
+    gather_y(1)
+    scatter_y(6)
+    gather_z(3)
+    multiply(7)
+    gather_core(0)
+    scatter_z(5)
+    scatter_y(7)
+    multiply(8)
+    gather_z(4)
+    gather_y(2)
+    gather_core(1)
+    multiply_back(0, 0)
+    gather_y(3)
+    scatter_z(6)
+    multiply_back(0, 1)
+    multiply_back(0, 2)
+    multiply_back(0, 3)
+    scatter_z(7)
+    multiply_back(1, 0)
+    multiply_back(1, 1)
+    gather_y(4)
+    scatter_z(8)
+    multiply_back(1, 2)
+    multiply_back(1, 3)
+    gather_y(5)
+    gather_y(6)
+    gather_core(2)
+    gather_y(7)
+    gather_core(3)
+    multiply_back(2, 0)
+    gather_y(8)
+    multiply_back(2, 1)
+    multiply_back(2, 2)
+    gather_core(4)
+    multiply_back(2, 3)
+    gather_core(5)
+    gather_core(6)
+    multiply_back(3, 0)
+    gather_core(7)
+    multiply_back(3, 1)
+    multiply_back(3, 2)
+    multiply_back(3, 3)
+    gather_core(8)
+    multiply_back(4, 0)
+    multiply_back(4, 1)
+    multiply_back(4, 2)
+    multiply_back(4, 3)
     for copy in unsent:
         copy.wait_send()
 
@@ -322,6 +392,7 @@
         out_specs=pl.BlockSpec(memory_space=pltpu.VMEM),
         scratch_shapes=[
             pltpu.VMEM((ROWS, COLS), BF16),
+            pltpu.VMEM((COLS, ROWS), BF16),
             pltpu.VMEM((ROWS, COLS), BF16),
             pltpu.VMEM((VEC, COLS), BF16),
             pltpu.VMEM((ROWS, COLS), F32),

time: 81 us -> 78.1 us (0.964)
  Pallas kernels: 78.8 us -> 76 us
    pallas_call x1, Pallas kernels: 78.8 us -> 76 us  [cycle_term(): pl.pallas_call(body, name='cycle_term', out_shape=pltpu.VMEM((ROWS, COLS)...]
where the time goes in v3:
time: 78.1 us; the launch traced here: 78 us
  Pallas kernels  76 us (97%)
  local copies, waits for them, and re-layouts  2.02 us (3%)
    pallas_call x1, Pallas kernels, cycle_term(): pl.pallas_call(body, name='cycle_term', out_shape=pltpu.VMEM((ROWS, COLS)...  76 us
    unnamed x1, local copies, waits for them, and re-layouts  2.02 us

profile of v3, /device:TPU:1, one launch (start us, length us, event | category | flops | bytes accessed | tf_op | source)
XLA Modules:
  0.0 78.0 jit_solution(2574115164009637145)
XLA Ops:
  0.0 76.0 %cycle_term.1 = bf16[1024,2048]{1,0:T(8,128)(2,1)S(1)} custom-call(bf16[1024,2048]{1,0:T(8,128)(2,1)} %a_hbm.1, bf16[1024,2048]{1,0:T(8,128)(2,1)} %r_hbm.1, bf16[160,2048]{1,0:T(8,128)(2,1)} %bitcast.1), custom_call_target="tpu_custom_call" | custom-call | flops 10737418240 | bytes 14680064 | tf_op jit(solution)/shard_map/cycle_term/pallas_call | solution.py:387
  76.0 2.0 %copy.5 = bf16[1024,2048]{1,0:T(8,128)(2,1)} copy(bf16[1024,2048]{1,0:T(8,128)(2,1)S(1)} %cycle_term.1) | data formatting | bytes 8388608

commit v4 on v3

--- a/solution.py
+++ b/solution.py
@@ -100,6 +100,10 @@
         unsent.append(copy)
         return copy
 
+    def drain(count):
+        for _ in range(count):
+            unsent.pop(0).wait_send()
+
     arriving = {}
 
     def move(piece, to, send_sem, recv_sem, device):
@@ -269,9 +273,9 @@
             s = pl.ds(t * LANES, LANES)
             update = jnp.dot(chi[t, rows, :].T, panel[rows, :], preferred_element_type=F32)
             if g == len(GROUPS) - 1:
-                out[s, :] = (res[s, :].astype(F32) + (acc[s, :] + update)).astype(BF16)
+                out[s, :] = (acc[s, :] + update).astype(BF16)
             elif g == 0:
-                acc[s, :] = update
+                acc[s, :] = res[s, :].astype(F32) + update
             else:
                 acc[s, :] += update
 
@@ -300,6 +304,7 @@
     crossed(2)
     crossed(3)
     multiply(1)
+    early = len(unsent)
     crossed(4)
     scatter_z(0)
     scatter_y(1)
@@ -314,6 +319,7 @@
     pass_on(5, 1)
     pass_on(6, 2)
     multiply(3)
+    drain(early)
     crossed(9)
     gather_z(0)
     scatter_y(3)
@@ -322,6 +328,7 @@
     scatter_z(2)
     gather_z(1)
     multiply(5)
+    middle = len(unsent)
     gather_y(0)
     scatter_z(3)
     scatter_y(5)
@@ -355,6 +362,7 @@
     multiply_back(1, 3)
     gather_y(5)
     gather_y(6)
+    drain(middle)
     gather_core(2)
     gather_y(7)
     gather_core(3)

time: 78.1 us -> 78 us (level)
  no operation moved by 1% of the time
where the time goes in v4:
time: 78 us
  Pallas kernels  75.9 us (97%)
  local copies, waits for them, and re-layouts  2.02 us (3%)
    pallas_call x1, Pallas kernels, cycle_term(): pl.pallas_call(body, name='cycle_term', out_shape=pltpu.VMEM((ROWS, COLS)...  75.9 us
    unnamed x1, local copies, waits for them, and re-layouts  2.02 us

profile of v4, /device:TPU:1, one launch (start us, length us, event | category | flops | bytes accessed | tf_op | source)
XLA Modules:
  0.0 78.0 jit_solution(6026009819667446301)
XLA Ops:
  0.0 75.9 %cycle_term.1 = bf16[1024,2048]{1,0:T(8,128)(2,1)S(1)} custom-call(bf16[1024,2048]{1,0:T(8,128)(2,1)} %a_hbm.1, bf16[1024,2048]{1,0:T(8,128)(2,1)} %r_hbm.1, bf16[160,2048]{1,0:T(8,128)(2,1)} %bitcast.1), custom_call_target="tpu_custom_call" | custom-call | flops 10737418240 | bytes 14680064 | tf_op jit(solution)/shard_map/cycle_term/pallas_call | solution.py:395
  75.9 2.0 %copy.5 = bf16[1024,2048]{1,0:T(8,128)(2,1)} copy(bf16[1024,2048]{1,0:T(8,128)(2,1)S(1)} %cycle_term.1) | data formatting | bytes 8388608
